TPU v7x, 32 devices: a whole 2x2x4 slice. The times are simulated.
32 devices in a mesh: groups: 2 (over x), frame: 16 (over z, y, core).
Axes of the slice: x: 2, y: 2, z: 4, core: 2. Of those that a mesh axis runs over, the one named last changes fastest.
Arguments:
- frames_in: bfloat16 [32, 256, 2240], P(('groups', 'frame')), parts along dimension 0, may hold values from -16 to 16
- qkv_weight: bfloat16 [3, 2240, 1280], P(None, None, 'frame'), may hold values from -0.125 to 0.125
Outputs:
- attended: bfloat16 [32, 256, 1280], P(('groups', 'frame')), parts along dimension 0
There are 2 independent parts, one for each index of `groups`. A program takes and returns all parts, laid end to end along the dimension named above; an argument that names none is the same for every part. Nothing has to cross between parts.
All inputs are finite; a program needn't handle non-finite values.
Results may differ from a plain program's by a relative error of at most 0.0039.
Values may be sent and summed in bfloat16 or wider, within the bound.
A program may use at most 128 MiB of HBM per device.

v0:
```python
import jax
import jax.numpy as jnp
from jax import lax
from jax.sharding import PartitionSpec as P

HEAD_DIM = 32
HEADS = 40
EPSILON = 1e-06


def entering(shard, axis, join, neutral):
    place = lax.axis_index(axis)
    gathered = jax.tree.map(
        lambda a, kind: lax.all_gather(a.astype(kind), axis), shard, (jnp.bfloat16, jnp.bfloat16)
    )
    state = jax.tree.map(lambda a, e: jnp.zeros_like(a) + jnp.asarray(e, a.dtype), shard, neutral)

    def one(hop, state):
        return join(
            state,
            jax.tree.map(
                lambda a, own: lax.dynamic_index_in_dim(a, hop, 0, False).astype(own.dtype),
                gathered,
                shard,
            ),
        )

    return lax.fori_loop(0, place, one, state)


def add_pair(earlier, later):
    return (earlier[0] + later[0], earlier[1] + later[1])


def carry_states(key_rows, value_rows):
    count = key_rows.shape[0]
    feature_k = jax.nn.relu(key_rows).reshape(count, HEADS, HEAD_DIM)
    values = value_rows.reshape(count, HEADS, HEAD_DIM)
    local_state = jnp.einsum("thi,thj->hij", feature_k, values, preferred_element_type=jnp.float32)
    local_keys = jnp.sum(feature_k.astype(jnp.float32), axis=0)
    prior_state, prior_keys = entering(
        (local_state, local_keys),
        "frame",
        add_pair,
        (jnp.zeros_like(local_state), jnp.zeros_like(local_keys)),
    )
    return (local_state, local_keys, prior_state, prior_keys)


def apply_state(feature_q, state, key_sum):
    numer = jnp.einsum("thi,hij->thj", feature_q, state, precision=lax.Precision.HIGHEST)
    denom = jnp.einsum("thi,hi->th", feature_q, key_sum, precision=lax.Precision.HIGHEST)
    return (numer, denom)


def shards(frames_in, qkv_weight):
    tokens = frames_in[0]
    count = tokens.shape[0]
    weights_all = lax.all_gather(qkv_weight, "frame", axis=2, tiled=True)
    projected = jnp.einsum("td,sdc->stc", tokens, weights_all, preferred_element_type=jnp.float32)
    queries = projected[0]
    key_rows = projected[1].astype(jnp.bfloat16)
    value_rows = projected[2].astype(jnp.bfloat16)
    local_state, local_keys, prior_state, prior_keys = carry_states(key_rows, value_rows)
    feature_q = jax.nn.relu(queries).reshape(count, HEADS, HEAD_DIM)
    own_numer, own_denom = apply_state(feature_q, local_state, local_keys)
    past_numer, past_denom = apply_state(feature_q, prior_state, prior_keys)
    numer = past_numer + own_numer
    denom = past_denom + own_denom
    attended = (numer / (denom[:, :, None] + EPSILON)).astype(jnp.bfloat16)
    return attended.reshape(1, count, HEADS * HEAD_DIM)


def solution(mesh):
    placed = (P(("groups", "frame"), None, None), P(None, None, "frame"))
    return jax.shard_map(
        shards,
        mesh=mesh,
        in_specs=placed,
        out_specs=P(("groups", "frame"), None, None),
        check_vma=False,
    )
```

profile of v0, /device:TPU:29, one launch (start us, length us, event | category | flops | bytes accessed | tf_op | source)
XLA Modules:
  0.0 198.7 jit_solution(12941034522131766999)
XLA Ops:
  6.5 0.0 copy-start
  6.5 0.0 all-gather.4.cloned.1.call-start
  6.5 0.7 all-gather.4.cloned.1.call-update
  7.3 0.0 all-gather.6.cloned.1.call-start
  7.3 95.5 %all-gather.4.cloned.1.call-done = bf16[3,2240,1280]{1,2,0:T(8,128)(2,1)} async-done(((bf16[3,2240,80]{1,2,0:T(8,128)(2,1)}), bf16[3,2240,1280]{1,2,0:T(8,128)(2,1)}) %all-gather.4.cloned.1.call-update) | async-done | bytes 17203216 | tf_op jit(solution)/shard_map/all_gather | solution.py:59
  102.8 0.0 copy-done
  102.8 8.5 %convolution_bitcast_fusion = f32[3,256,1280]{1,2,0:T(8,128)S(1)} fusion(bf16[3,2240,1280]{1,2,0:T(8,128)(2,1)} %all-gather.4.cloned.1.call-done, bf16[1,256,2240]{1,2,0:T(8,128)(2,1)S(1)} %copy-done), kind=kOutput, calls=%fused_computation.3 | convolution fusion | flops 4404019200 | bytes 22282240 | tf_op jit(solution)/shard_map/td,sdc->stc/dot_general | solution.py:60
  111.3 0.3 convert_reduce_fusion
  111.6 0.1 slice.21
  111.6 1.3 fusion.8
  112.9 0.0 all-gather.6.cloned.1.call-update
  113.0 0.1 reshape.41
  113.0 0.1 convert_element_type.51
  113.1 0.1 copy.9
  113.2 17.0 %all_gather.16 = bf16[16,40,32]{1,2,0:T(8,128)(2,1)S(1)} all-gather(bf16[1,40,32]{1,2,0:T(8,128)(2,1)S(1)} %copy.9), channel_id=1, replica_groups=mesh['groups'=2,'frame'=16] {'frame'}, dimensions={0}, use_global_device_ids=true | all-gather | bytes 43520 | tf_op jit(solution)/shard_map/all_gather | solution.py:14
  130.2 0.8 fusion.11
  130.9 37.0 %all-gather.6.cloned.1.call-done = bf16[640,32,32]{2,1,0:T(8,128)(2,1)} async-done(((bf16[40,32,32]{2,1,0:T(8,128)(2,1)}), bf16[640,32,32]{2,1,0:T(8,128)(2,1)}) %all-gather.6.cloned.1.call-update) | async-done | bytes 1310736 | tf_op jit(solution)/shard_map/all_gather | solution.py:14
  168.0 0.1 broadcast_in_dim.7
  168.1 19.2 %while.12 = (s32[]{:T(128)}, f32[40,32,32]{2,1,0:T(8,128)S(1)}, f32[40,32]{1,0:T(8,128)S(1)}, s32[]{:T(128)}, bf16[16,40,32,32]{3,2,1,0:T(8,128)(2,1)}, /*index=...) while((s32[]{:T(128)}, f32[40,32,32]{2,1,0:T(8,128)S(1)}, f32[40,32]{1,0:T(8,128)S(1)}, ...), condition=%wide.region_2.3_spmd, body=%wide.region_1.2_spmd.sunk | while | flops 84485 | bytes 432775 | solution.py:28
  168.1 1.1 convert_add_fusion.4
  169.2 0.1 copy.24
  169.4 1.1 convert_add_fusion.4
  170.5 0.1 copy.24
  170.6 1.1 convert_add_fusion.4
  171.8 0.1 copy.24
  171.9 1.1 convert_add_fusion.4
  173.1 0.1 copy.24
  173.2 1.1 convert_add_fusion.4
  174.4 0.1 copy.24
  174.5 1.1 convert_add_fusion.4
  175.6 0.1 copy.24
  175.8 1.1 convert_add_fusion.4
  176.9 0.1 copy.24
  177.0 1.1 convert_add_fusion.4
  178.2 0.1 copy.24
  178.3 1.1 convert_add_fusion.4
  179.5 0.1 copy.24
  179.6 1.1 convert_add_fusion.4
  180.8 0.1 copy.24
  180.9 1.1 convert_add_fusion.4
  182.0 0.1 copy.24
  182.2 1.1 convert_add_fusion.4
  183.3 0.1 copy.24
  183.4 1.1 convert_add_fusion.4
  184.6 0.1 copy.24
  184.7 1.1 convert_add_fusion.4
  185.9 0.1 copy.24
  186.0 1.1 convert_add_fusion.4
  187.2 0.1 copy.24
  187.3 0.8 fusion.10
  188.0 0.0 copy-start.1
  188.0 1.3 fusion.9
  189.4 0.0 copy-done.1
  189.4 1.4 fusion.2
  190.8 1.1 copy.13
  (33 shorter events, 0.3 us)
Async XLA Ops:
  6.5 96.2 %copy-start = (bf16[1,256,2240]{1,2,0:T(8,128)(2,1)S(1)}, bf16[1,256,2240]{1,2,0:T(8,128)(2,1)}, u32[]{:S(2)}) copy-start(bf16[1,256,2240]{1,2,0:T(8,128)(2,1)} %param.4) | copy-start | bytes 3440644
  6.5 96.2 %all-gather.4.cloned.1.call-start = ((), (), s32[]{:S(2)}) async-start(), calls=%async_computation | async-start | bytes 18800640 | tf_op jit(solution)/shard_map/all_gather | solution.py:59
  7.3 160.7 %all-gather.6.cloned.1.call-start = ((), (), s32[]{:S(2)}) async-start(), calls=%async_computation.1 | async-start | bytes 5570560 | tf_op jit(solution)/shard_map/all_gather | solution.py:14
  188.0 1.4 copy-start.1
Sparse Core Ops, SparseCore 0:
  8.9 93.8 all-gather.3
  113.1 54.8 all-gather.5
where the time goes:
time: 199 us
  waiting for transfers between devices  133 us (67%)
  other arithmetic  17.4 us (9%)
  blocking collectives  17 us (9%)
  matrix products  14 us (7%)
  between operations  13.5 us (7%)
  local copies, waits for them, and re-layouts  2.92 us (1%)
    all_gather x1, waiting for transfers between devices, shards(): weights_all = lax.all_gather(qkv_weight, 'frame', axis=2, tiled=True)  95.5 us
    all_gather x1, waiting for transfers between devices, entering(): lax.all_gather(a.astype(kind), axis)  37 us
    add x30, other arithmetic, add_pair(): return (earlier[0] + later[0], earlier[1] + later[1])  17.2 us
    all_gather x1, blocking collectives, entering(): lax.all_gather(a.astype(kind), axis)  17 us
    dot_general x1, matrix products, shards(): jnp.einsum('td,sdc->stc', tokens, weights_all, preferred_element_type=jnp...  8.53 us
  transfers between devices with their start and end apart: 2, of which 2 were waited for; matrix products, arithmetic and copies ran while one was open for 1% of the time, Pallas kernels for 0%

commit v1 on v0

--- a/solution.py
+++ b/solution.py
@@ -6,6 +6,31 @@
 HEAD_DIM = 32
 HEADS = 40
 EPSILON = 1e-06
+
+
+def in_order(tiles, dim):
+    tiles = jnp.moveaxis(tiles, 0, dim)
+    dims = tiles.shape
+    return tiles.reshape(*dims[:dim], dims[dim] * dims[dim + 1], *dims[dim + 2 :])
+
+
+def on_each_block(x, axis, dim, apply, out_dim):
+    size, place, extent = (lax.axis_size(axis), lax.axis_index(axis), x.shape[dim])
+    right = [(i, (i + 1) % size) for i in range(size)]
+    backward = [(i, (i - 1) % size) for i in range(size)]
+    half = size // 2
+    blocks = {}
+    from_left = from_right = x
+    for step in range(half + 1):
+        next_left = lax.ppermute(from_left, axis, right) if step < half else None
+        next_right = lax.ppermute(from_right, axis, backward) if step < size - half - 1 else None
+        blocks[-step] = apply(from_left, (place - step) % size * extent)
+        if 0 < step < size - half:
+            blocks[step] = apply(from_right, (place + step) % size * extent)
+        from_left, from_right = (next_left, next_right)
+    blocks = jnp.stack([blocks[k] for k in sorted(blocks)])
+    blocks = blocks[(jnp.arange(size) - place + half) % size]
+    return in_order(blocks, out_dim)
 
 
 def entering(shard, axis, join, neutral):
@@ -56,8 +81,15 @@
 def shards(frames_in, qkv_weight):
     tokens = frames_in[0]
     count = tokens.shape[0]
-    weights_all = lax.all_gather(qkv_weight, "frame", axis=2, tiled=True)
-    projected = jnp.einsum("td,sdc->stc", tokens, weights_all, preferred_element_type=jnp.float32)
+    projected = on_each_block(
+        qkv_weight,
+        "frame",
+        2,
+        lambda shard_2, at: jnp.einsum(
+            "td,sdc->stc", tokens, shard_2, preferred_element_type=jnp.float32
+        ),
+        2,
+    )
     queries = projected[0]
     key_rows = projected[1].astype(jnp.bfloat16)
     value_rows = projected[2].astype(jnp.bfloat16)

time: 199 us -> 324 us (1.63)
  starting transfers between devices: 0.04 us -> 140 us
  waiting for transfers between devices: 133 us -> 77.2 us
  matrix products: 14 us -> 29.1 us
  blocking collectives: 17 us -> 32.1 us
  local copies, waits for them, and re-layouts: 2.92 us -> 10.7 us
    ppermute x0 -> x15, starting transfers between devices: none -> 140 us  [the longest x7 130 us: on_each_block(): lax.ppermute(from_right, axis, backward)]
    all_gather x1 -> x0, waiting for transfers between devices: 95.5 us -> none  [shards(): weights_all = lax.all_gather(qkv_weight, 'frame', axis=2, tiled=True)]
    ppermute x0 -> x15, waiting for transfers between devices: none -> 40.2 us  [the longest x8 25 us: on_each_block(): next_left = lax.ppermute(from_left, axis, right) if step < half else None]
    dot_general x1 -> x16, matrix products: 8.53 us -> 23.7 us  [shards(): jnp.einsum('td,sdc->stc', tokens, shard_2, preferred_element_type=jnp.flo...]
    all_gather x1, blocking collectives: 17 us -> 32.1 us  [entering(): lax.all_gather(a.astype(kind), axis)]
    gather x0 -> x1, local copies, waits for them, and re-layouts: none -> 4.81 us  [on_each_block(): blocks = blocks[(jnp.arange(size) - place + half) % size]]
  transfers between devices with their start and end apart: 2 -> 16, of which waited for: 2 -> 9; matrix products, arithmetic and copies ran while one was open for 1% -> 7% of each run, Pallas kernels for 0% -> 0%
where the time goes in v1:
time: 324 us; the launch traced here: 323 us
  starting transfers between devices  140 us (43%)
  waiting for transfers between devices  77.2 us (24%)
  blocking collectives  32.1 us (10%)
  matrix products  29.1 us (9%)
  other arithmetic  19.3 us (6%)
  between operations  13.6 us (4%)
  local copies, waits for them, and re-layouts  10.7 us (3%)
    ppermute x7, starting transfers between devices, on_each_block(): lax.ppermute(from_right, axis, backward)  130 us
    all_gather x1, waiting for transfers between devices, entering(): lax.all_gather(a.astype(kind), axis)  37 us
    all_gather x1, blocking collectives, entering(): lax.all_gather(a.astype(kind), axis)  32.1 us
    ppermute x8, waiting for transfers between devices, on_each_block(): next_left = lax.ppermute(from_left, axis, right) if step < half else None  25 us
    dot_general x16, matrix products, shards(): jnp.einsum('td,sdc->stc', tokens, shard_2, preferred_element_type=jnp.flo...  23.7 us
    add x30, other arithmetic, add_pair(): return (earlier[0] + later[0], earlier[1] + later[1])  17.2 us
    ppermute x7, waiting for transfers between devices, on_each_block(): lax.ppermute(from_right, axis, backward)  15.1 us
    ppermute x8, starting transfers between devices, on_each_block(): next_left = lax.ppermute(from_left, axis, right) if step < half else None  10.5 us
  transfers between devices with their start and end apart: 16, of which 9 were waited for; matrix products, arithmetic and copies ran while one was open for 7% of the time, Pallas kernels for 0%

profile of v1, /device:TPU:29, one launch (start us, length us, event | category | flops | bytes accessed | tf_op | source)
XLA Modules:
  0.0 322.8 jit_solution(1313676111004343440)
XLA Ops:
  6.5 12.7 %collective-permute-done = bf16[3,2240,80]{1,2,0:T(8,128)(2,1)S(1)} collective-permute-done((bf16[3,2240,80]{1,2,0:T(8,128)(2,1)}, bf16[3,2240,80]{1,2,0:T(8,128)(2,1)S(1)}, u32[]{:S(2)}, u32[]{:S(2)}) %collective-permute-start) | collective-permute-done | bytes 1075232 | tf_op jit(solution)/shard_map/ppermute | solution.py:25
  19.2 5.1 %collective-permute-start.1 = (bf16[3,2240,80]{1,2,0:T(8,128)(2,1)S(1)}, bf16[3,2240,80]{1,2,0:T(8,128)(2,1)S(1)}, u32[]{:S(2)}, u32[]{:S(2)}) collective-permute-start(bf16[3,2240,80]{1,2,0:T(8,128)(2,1)S(1)} %collective-permute-done), channel_id=1, source_target_pairs={{0,1},{1,2},{2,3},{3,4},{4,5},{5,6},{6,7},{7,8},{8,9},{9,10},{10,1... | collective-permute-start | bytes 3225608 | tf_op jit(solution)/shard_map/ppermute | solution.py:25
  24.3 12.4 %collective-permute-done.1 = bf16[3,2240,80]{1,2,0:T(8,128)(2,1)S(1)} collective-permute-done((bf16[3,2240,80]{1,2,0:T(8,128)(2,1)S(1)}, bf16[3,2240,80]{1,2,0:T(8,128)(2,1)S(1)}, u32[]{:S(2)}, u32[]{:S(2)}) %collective-permute-start.1) | collective-permute-done | bytes 1075232 | tf_op jit(solution)/shard_map/ppermute | solution.py:25
  36.6 5.3 %collective-permute-start.2 = (bf16[3,2240,80]{1,2,0:T(8,128)(2,1)S(1)}, bf16[3,2240,80]{1,2,0:T(8,128)(2,1)S(1)}, u32[]{:S(2)}, u32[]{:S(2)}) collective-permute-start(bf16[3,2240,80]{1,2,0:T(8,128)(2,1)S(1)} %collective-permute-done.1), channel_id=1, source_target_pairs={{0,1},{1,2},{2,3},{3,4},{4,5},{5,6},{6,7},{7,8},{8,9},{9,10},{10,1... | collective-permute-start | bytes 3225608 | tf_op jit(solution)/shard_map/ppermute | solution.py:25
  41.9 0.2 collective-permute-done.8
  42.1 18.6 %collective-permute-start.9 = (bf16[3,2240,80]{1,2,0:T(8,128)(2,1)S(1)}, bf16[3,2240,80]{1,2,0:T(8,128)(2,1)S(1)}, u32[]{:S(2)}, u32[]{:S(2)}) collective-permute-start(bf16[3,2240,80]{1,2,0:T(8,128)(2,1)S(1)} %collective-permute-done.8), channel_id=1, source_target_pairs={{0,15},{1,0},{2,1},{3,2},{4,3},{5,4},{6,5},{7,6},{8,7},{9,8},{10,9... | collective-permute-start | bytes 3225608 | tf_op jit(solution)/shard_map/ppermute | solution.py:26
  60.7 2.4 collective-permute-done.9
  63.1 22.1 %collective-permute-start.10 = (bf16[3,2240,80]{1,2,0:T(8,128)(2,1)S(1)}, bf16[3,2240,80]{1,2,0:T(8,128)(2,1)S(1)}, u32[]{:S(2)}, u32[]{:S(2)}) collective-permute-start(bf16[3,2240,80]{1,2,0:T(8,128)(2,1)S(1)} %collective-permute-done.9), channel_id=1, source_target_pairs={{0,15},{1,0},{2,1},{3,2},{4,3},{5,4},{6,5},{7,6},{8,7},{9,8},{10,9... | collective-permute-start | bytes 3225608 | tf_op jit(solution)/shard_map/ppermute | solution.py:26
  85.3 2.3 collective-permute-done.10
  87.6 22.2 %collective-permute-start.11 = (bf16[3,2240,80]{1,2,0:T(8,128)(2,1)S(1)}, bf16[3,2240,80]{1,2,0:T(8,128)(2,1)S(1)}, u32[]{:S(2)}, u32[]{:S(2)}) collective-permute-start(bf16[3,2240,80]{1,2,0:T(8,128)(2,1)S(1)} %collective-permute-done.10), channel_id=1, source_target_pairs={{0,15},{1,0},{2,1},{3,2},{4,3},{5,4},{6,5},{7,6},{8,7},{9,8},{10,9... | collective-permute-start | bytes 3225608 | tf_op jit(solution)/shard_map/ppermute | solution.py:26
  109.9 3.2 collective-permute-done.11
  113.0 1.0 copy-done.10
  114.0 21.5 %collective-permute-start.12 = (bf16[3,2240,80]{1,2,0:T(8,128)(2,1)S(1)}, bf16[3,2240,80]{1,2,0:T(8,128)(2,1)}, u32[]{:S(2)}, u32[]{:S(2)}) collective-permute-start(bf16[3,2240,80]{1,2,0:T(8,128)(2,1)S(1)} %collective-permute-done.11), channel_id=1, source_target_pairs={{0,15},{1,0},{2,1},{3,2},{4,3},{5,4},{6,5},{7,6},{8,7},{9,8},{10,9... | collective-permute-start | bytes 3225608 | tf_op jit(solution)/shard_map/ppermute | solution.py:26
  135.6 4.5 %collective-permute-done.12 = bf16[3,2240,80]{1,2,0:T(8,128)(2,1)} collective-permute-done((bf16[3,2240,80]{1,2,0:T(8,128)(2,1)S(1)}, bf16[3,2240,80]{1,2,0:T(8,128)(2,1)}, u32[]{:S(2)}, u32[]{:S(2)}) %collective-permute-start.12) | collective-permute-done | bytes 1075232 | tf_op jit(solution)/shard_map/ppermute | solution.py:26
  140.0 22.1 %collective-permute-start.13 = (bf16[3,2240,80]{1,2,0:T(8,128)(2,1)}, bf16[3,2240,80]{1,2,0:T(8,128)(2,1)}, u32[]{:S(2)}, u32[]{:S(2)}) collective-permute-start(bf16[3,2240,80]{1,2,0:T(8,128)(2,1)} %collective-permute-done.12), channel_id=1, source_target_pairs={{0,15},{1,0},{2,1},{3,2},{4,3},{5,4},{6,5},{7,6},{8,7},{9,8},{10,9... | collective-permute-start | bytes 3225608 | tf_op jit(solution)/shard_map/ppermute | solution.py:26
  162.2 2.6 collective-permute-done.13
  164.8 23.0 %collective-permute-start.14 = (bf16[3,2240,80]{1,2,0:T(8,128)(2,1)}, bf16[3,2240,80]{1,2,0:T(8,128)(2,1)S(1)}, u32[]{:S(2)}, u32[]{:S(2)}) collective-permute-start(bf16[3,2240,80]{1,2,0:T(8,128)(2,1)} %collective-permute-done.13), channel_id=1, source_target_pairs={{0,15},{1,0},{2,1},{3,2},{4,3},{5,4},{6,5},{7,6},{8,7},{9,8},{10,9... | collective-permute-start | bytes 3225608 | tf_op jit(solution)/shard_map/ppermute | solution.py:26
  187.9 2.4 fusion.18
  190.2 2.5 fusion.17
  192.7 1.2 fusion.16
  194.0 1.2 fusion.15
  195.2 1.2 fusion.14
  196.5 1.2 fusion.13
  197.7 1.2 fusion.12
  198.9 1.2 fusion.11
  200.1 0.1 copy-done.1
  200.1 1.2 fusion.10
  201.3 1.2 fusion.9
  202.6 1.2 fusion.8
  203.8 1.2 fusion.7
  205.0 1.2 fusion.6
  206.2 2.4 fusion.5
  208.6 2.4 fusion.4
  211.0 1.2 fusion.3
  212.1 4.8 %gather_fusion = f32[16,3,256,80]{2,3,1,0:T(8,128)} fusion(f32[16,3,256,80]{2,3,1,0:T(8,128)} %fusion.3, s32[1024]{0:T(1024)S(1)} %pad_clamp_fusion), kind=kCustom, calls=%fused_computation | custom fusion | bytes 7864384 | tf_op jit(solution)/shard_map/gather | solution.py:32
  216.9 2.1 convert_reduce_fusion
  219.1 1.4 slice.26
  220.5 1.3 fusion.41
  221.8 0.1 convert_element_type.51
  222.0 32.1 %all_gather.12 = bf16[16,40,32]{1,2,0:T(8,128)(2,1)S(1)} all-gather(bf16[1,40,32]{1,2,0:T(8,128)(2,1)S(1)} %copy.9), channel_id=1, replica_groups=mesh['groups'=2,'frame'=16] {'frame'}, dimensions={0}, use_global_device_ids=true | all-gather | bytes 43520 | tf_op jit(solution)/shard_map/all_gather | solution.py:39
  254.1 0.8 fusion.44
  254.8 37.0 %all-gather.3.cloned.1.call-done = bf16[640,32,32]{2,1,0:T(8,128)(2,1)} async-done(((bf16[40,32,32]{2,1,0:T(8,128)(2,1)}), bf16[640,32,32]{2,1,0:T(8,128)(2,1)}) %all-gather.3.cloned.1.call-update) | async-done | bytes 1310736 | tf_op jit(solution)/shard_map/all_gather | solution.py:39
  292.0 19.4 %while.12 = (s32[]{:T(128)}, f32[40,32,32]{2,1,0:T(8,128)S(1)}, f32[40,32]{1,0:T(8,128)S(1)}, s32[]{:T(128)}, bf16[16,40,32,32]{3,2,1,0:T(8,128)(2,1)}, /*index=...) while((s32[]{:T(128)}, f32[40,32,32]{2,1,0:T(8,128)S(1)}, f32[40,32]{1,0:T(8,128)S(1)}, ...), condition=%wide.region_2.3_spmd, body=%wide.region_1.2_spmd.sunk | while | flops 84485 | bytes 432775 | solution.py:53
  292.0 1.1 convert_add_fusion.4
  293.1 0.1 copy.24
  293.3 1.1 convert_add_fusion.4
  294.6 1.1 convert_add_fusion.4
  295.8 1.1 convert_add_fusion.4
  297.1 1.1 convert_add_fusion.4
  298.4 1.1 convert_add_fusion.4
  299.7 1.1 convert_add_fusion.4
  301.0 1.1 convert_add_fusion.4
  302.1 0.1 copy.24
  302.2 1.1 convert_add_fusion.4
  303.5 1.1 convert_add_fusion.4
  304.8 1.1 convert_add_fusion.4
  306.1 1.1 convert_add_fusion.4
  307.4 1.1 convert_add_fusion.4
  308.6 1.1 convert_add_fusion.4
  309.9 1.1 convert_add_fusion.4
  311.4 0.8 fusion.43
  312.1 1.3 fusion.42
  313.4 1.4 fusion.2
  314.9 1.1 copy.13
  (103 shorter events, 2.4 us)
Async XLA Ops:
  6.5 181.3 %copy-start = (bf16[1,256,2240]{1,2,0:T(8,128)(2,1)S(1)}, bf16[1,256,2240]{1,2,0:T(8,128)(2,1)}, u32[]{:S(2)}) copy-start(bf16[1,256,2240]{1,2,0:T(8,128)(2,1)} %param.4) | copy-start | bytes 3440644
  6.5 285.3 %all-gather.3.cloned.1.call-start = ((), (), s32[]{:S(2)}) async-start(), calls=%async_computation | async-start | bytes 5570560 | tf_op jit(solution)/shard_map/all_gather | solution.py:39
  6.5 12.7 %collective-permute-start = (bf16[3,2240,80]{1,2,0:T(8,128)(2,1)}, bf16[3,2240,80]{1,2,0:T(8,128)(2,1)S(1)}, u32[]{:S(2)}, u32[]{:S(2)}) collective-permute-start(bf16[3,2240,80]{1,2,0:T(8,128)(2,1)} %param.5), channel_id=1, source_target_pairs={{0,1},{1,2},{2,3},{3,4},{4,5},{5,6},{6,7},{7,8},{8,9},{9,10},{10,1... | collective-permute-start | bytes 3225608 | tf_op jit(solution)/shard_map/ppermute | solution.py:25
  19.2 17.4 %collective-permute-start.1 = (bf16[3,2240,80]{1,2,0:T(8,128)(2,1)S(1)}, bf16[3,2240,80]{1,2,0:T(8,128)(2,1)S(1)}, u32[]{:S(2)}, u32[]{:S(2)}) collective-permute-start(bf16[3,2240,80]{1,2,0:T(8,128)(2,1)S(1)} %collective-permute-done), channel_id=1, source_target_pairs={{0,1},{1,2},{2,3},{3,4},{4,5},{5,6},{6,7},{7,8},{8,9},{9,10},{10,1... | collective-permute-start | bytes 3225608 | tf_op jit(solution)/shard_map/ppermute | solution.py:25
  24.3 17.9 %collective-permute-start.8 = (bf16[3,2240,80]{1,2,0:T(8,128)(2,1)}, bf16[3,2240,80]{1,2,0:T(8,128)(2,1)S(1)}, u32[]{:S(2)}, u32[]{:S(2)}) collective-permute-start(bf16[3,2240,80]{1,2,0:T(8,128)(2,1)} %param.5), channel_id=1, source_target_pairs={{0,15},{1,0},{2,1},{3,2},{4,3},{5,4},{6,5},{7,6},{8,7},{9,8},{10,9... | collective-permute-start | bytes 3225608 | tf_op jit(solution)/shard_map/ppermute | solution.py:26
  36.6 26.5 %copy-start.2 = (bf16[3,2240,80]{1,2,0:T(8,128)(2,1)}, bf16[3,2240,80]{1,2,0:T(8,128)(2,1)S(1)}, u32[]{:S(2)}) copy-start(bf16[3,2240,80]{1,2,0:T(8,128)(2,1)S(1)} %collective-permute-done.1) | copy-start | bytes 3225604
  36.6 24.1 %collective-permute-start.2 = (bf16[3,2240,80]{1,2,0:T(8,128)(2,1)S(1)}, bf16[3,2240,80]{1,2,0:T(8,128)(2,1)S(1)}, u32[]{:S(2)}, u32[]{:S(2)}) collective-permute-start(bf16[3,2240,80]{1,2,0:T(8,128)(2,1)S(1)} %collective-permute-done.1), channel_id=1, source_target_pairs={{0,1},{1,2},{2,3},{3,4},{4,5},{5,6},{6,7},{7,8},{8,9},{9,10},{10,1... | collective-permute-start | bytes 3225608 | tf_op jit(solution)/shard_map/ppermute | solution.py:25
  42.1 21.0 %collective-permute-start.9 = (bf16[3,2240,80]{1,2,0:T(8,128)(2,1)S(1)}, bf16[3,2240,80]{1,2,0:T(8,128)(2,1)S(1)}, u32[]{:S(2)}, u32[]{:S(2)}) collective-permute-start(bf16[3,2240,80]{1,2,0:T(8,128)(2,1)S(1)} %collective-permute-done.8), channel_id=1, source_target_pairs={{0,15},{1,0},{2,1},{3,2},{4,3},{5,4},{6,5},{7,6},{8,7},{9,8},{10,9... | collective-permute-start | bytes 3225608 | tf_op jit(solution)/shard_map/ppermute | solution.py:26
  60.7 26.9 %copy-start.6 = (bf16[3,2240,80]{1,2,0:T(8,128)(2,1)}, bf16[3,2240,80]{1,2,0:T(8,128)(2,1)S(1)}, u32[]{:S(2)}) copy-start(bf16[3,2240,80]{1,2,0:T(8,128)(2,1)S(1)} %collective-permute-done.2) | copy-start | bytes 3225604
  60.7 24.5 %collective-permute-start.3 = (bf16[3,2240,80]{1,2,0:T(8,128)(2,1)S(1)}, bf16[3,2240,80]{1,2,0:T(8,128)(2,1)S(1)}, u32[]{:S(2)}, u32[]{:S(2)}) collective-permute-start(bf16[3,2240,80]{1,2,0:T(8,128)(2,1)S(1)} %collective-permute-done.2), channel_id=1, source_target_pairs={{0,1},{1,2},{2,3},{3,4},{4,5},{5,6},{6,7},{7,8},{8,9},{9,10},{10,1... | collective-permute-start | bytes 3225608 | tf_op jit(solution)/shard_map/ppermute | solution.py:25
  63.1 22.1 %copy-start.4 = (bf16[3,2240,80]{1,2,0:T(8,128)(2,1)}, bf16[3,2240,80]{1,2,0:T(8,128)(2,1)S(1)}, u32[]{:S(2)}) copy-start(bf16[3,2240,80]{1,2,0:T(8,128)(2,1)S(1)} %collective-permute-done.9) | copy-start | bytes 3225604
  63.1 24.5 %collective-permute-start.10 = (bf16[3,2240,80]{1,2,0:T(8,128)(2,1)S(1)}, bf16[3,2240,80]{1,2,0:T(8,128)(2,1)S(1)}, u32[]{:S(2)}, u32[]{:S(2)}) collective-permute-start(bf16[3,2240,80]{1,2,0:T(8,128)(2,1)S(1)} %collective-permute-done.9), channel_id=1, source_target_pairs={{0,15},{1,0},{2,1},{3,2},{4,3},{5,4},{6,5},{7,6},{8,7},{9,8},{10,9... | collective-permute-start | bytes 3225608 | tf_op jit(solution)/shard_map/ppermute | solution.py:26
  85.2 54.8 %copy-start.12 = (bf16[3,2240,80]{1,2,0:T(8,128)(2,1)}, bf16[3,2240,80]{1,2,0:T(8,128)(2,1)S(1)}, u32[]{:S(2)}) copy-start(bf16[3,2240,80]{1,2,0:T(8,128)(2,1)S(1)} %collective-permute-done.3) | copy-start | bytes 3225604
  85.2 24.6 %collective-permute-start.4 = (bf16[3,2240,80]{1,2,0:T(8,128)(2,1)S(1)}, bf16[3,2240,80]{1,2,0:T(8,128)(2,1)S(1)}, u32[]{:S(2)}, u32[]{:S(2)}) collective-permute-start(bf16[3,2240,80]{1,2,0:T(8,128)(2,1)S(1)} %collective-permute-done.3), channel_id=1, source_target_pairs={{0,1},{1,2},{2,3},{3,4},{4,5},{5,6},{6,7},{7,8},{8,9},{9,10},{10,1... | collective-permute-start | bytes 3225608 | tf_op jit(solution)/shard_map/ppermute | solution.py:25
  87.6 22.2 %copy-start.8 = (bf16[3,2240,80]{1,2,0:T(8,128)(2,1)}, bf16[3,2240,80]{1,2,0:T(8,128)(2,1)S(1)}, u32[]{:S(2)}) copy-start(bf16[3,2240,80]{1,2,0:T(8,128)(2,1)S(1)} %collective-permute-done.10) | copy-start | bytes 3225604
  87.6 25.4 %collective-permute-start.11 = (bf16[3,2240,80]{1,2,0:T(8,128)(2,1)S(1)}, bf16[3,2240,80]{1,2,0:T(8,128)(2,1)S(1)}, u32[]{:S(2)}, u32[]{:S(2)}) collective-permute-start(bf16[3,2240,80]{1,2,0:T(8,128)(2,1)S(1)} %collective-permute-done.10), channel_id=1, source_target_pairs={{0,15},{1,0},{2,1},{3,2},{4,3},{5,4},{6,5},{7,6},{8,7},{9,8},{10,9... | collective-permute-start | bytes 3225608 | tf_op jit(solution)/shard_map/ppermute | solution.py:26
  109.8 52.3 %copy-start.14 = (bf16[3,2240,80]{1,2,0:T(8,128)(2,1)}, bf16[3,2240,80]{1,2,0:T(8,128)(2,1)S(1)}, u32[]{:S(2)}) copy-start(bf16[3,2240,80]{1,2,0:T(8,128)(2,1)S(1)} %collective-permute-done.4) | copy-start | bytes 3225604
  109.8 25.7 %collective-permute-start.5 = (bf16[3,2240,80]{1,2,0:T(8,128)(2,1)S(1)}, bf16[3,2240,80]{1,2,0:T(8,128)(2,1)S(1)}, u32[]{:S(2)}, u32[]{:S(2)}) collective-permute-start(bf16[3,2240,80]{1,2,0:T(8,128)(2,1)S(1)} %collective-permute-done.4), channel_id=1, source_target_pairs={{0,1},{1,2},{2,3},{3,4},{4,5},{5,6},{6,7},{7,8},{8,9},{9,10},{10,1... | collective-permute-start | bytes 3225608 | tf_op jit(solution)/shard_map/ppermute | solution.py:25
  113.0 1.0 copy-start.10
  114.0 26.0 %collective-permute-start.12 = (bf16[3,2240,80]{1,2,0:T(8,128)(2,1)S(1)}, bf16[3,2240,80]{1,2,0:T(8,128)(2,1)}, u32[]{:S(2)}, u32[]{:S(2)}) collective-permute-start(bf16[3,2240,80]{1,2,0:T(8,128)(2,1)S(1)} %collective-permute-done.11), channel_id=1, source_target_pairs={{0,15},{1,0},{2,1},{3,2},{4,3},{5,4},{6,5},{7,6},{8,7},{9,8},{10,9... | collective-permute-start | bytes 3225608 | tf_op jit(solution)/shard_map/ppermute | solution.py:26
  135.5 26.6 %copy-start.16 = (bf16[3,2240,80]{1,2,0:T(8,128)(2,1)}, bf16[3,2240,80]{1,2,0:T(8,128)(2,1)S(1)}, u32[]{:S(2)}) copy-start(bf16[3,2240,80]{1,2,0:T(8,128)(2,1)S(1)} %collective-permute-done.5) | copy-start | bytes 3225604
  135.5 26.6 %collective-permute-start.6 = (bf16[3,2240,80]{1,2,0:T(8,128)(2,1)S(1)}, bf16[3,2240,80]{1,2,0:T(8,128)(2,1)}, u32[]{:S(2)}, u32[]{:S(2)}) collective-permute-start(bf16[3,2240,80]{1,2,0:T(8,128)(2,1)S(1)} %collective-permute-done.5), channel_id=1, source_target_pairs={{0,1},{1,2},{2,3},{3,4},{4,5},{5,6},{6,7},{7,8},{8,9},{9,10},{10,1... | collective-permute-start | bytes 3225608 | tf_op jit(solution)/shard_map/ppermute | solution.py:25
  140.0 24.8 %collective-permute-start.13 = (bf16[3,2240,80]{1,2,0:T(8,128)(2,1)}, bf16[3,2240,80]{1,2,0:T(8,128)(2,1)}, u32[]{:S(2)}, u32[]{:S(2)}) collective-permute-start(bf16[3,2240,80]{1,2,0:T(8,128)(2,1)} %collective-permute-done.12), channel_id=1, source_target_pairs={{0,15},{1,0},{2,1},{3,2},{4,3},{5,4},{6,5},{7,6},{8,7},{9,8},{10,9... | collective-permute-start | bytes 3225608 | tf_op jit(solution)/shard_map/ppermute | solution.py:26
  162.1 25.7 %collective-permute-start.7 = (bf16[3,2240,80]{1,2,0:T(8,128)(2,1)}, bf16[3,2240,80]{1,2,0:T(8,128)(2,1)}, u32[]{:S(2)}, u32[]{:S(2)}) collective-permute-start(bf16[3,2240,80]{1,2,0:T(8,128)(2,1)} %collective-permute-done.6), channel_id=1, source_target_pairs={{0,1},{1,2},{2,3},{3,4},{4,5},{5,6},{6,7},{7,8},{8,9},{9,10},{10,1... | collective-permute-start | bytes 3225608 | tf_op jit(solution)/shard_map/ppermute | solution.py:25
  164.8 46.1 %collective-permute-start.14 = (bf16[3,2240,80]{1,2,0:T(8,128)(2,1)}, bf16[3,2240,80]{1,2,0:T(8,128)(2,1)S(1)}, u32[]{:S(2)}, u32[]{:S(2)}) collective-permute-start(bf16[3,2240,80]{1,2,0:T(8,128)(2,1)} %collective-permute-done.13), channel_id=1, source_target_pairs={{0,15},{1,0},{2,1},{3,2},{4,3},{5,4},{6,5},{7,6},{8,7},{9,8},{10,9... | collective-permute-start | bytes 3225608 | tf_op jit(solution)/shard_map/ppermute | solution.py:26
  190.2 2.5 copy-start.17
  192.7 1.2 copy-start.15
  194.0 1.2 copy-start.13
  195.2 1.2 copy-start.7
  196.5 1.2 copy-start.3
  198.9 1.2 copy-start.1
  201.3 1.2 copy-start.5
  202.5 1.2 copy-start.9
  203.8 1.2 copy-start.11
  312.1 1.3 copy-start.18
Sparse Core Ops, SparseCore 0:
  221.9 69.9 all-gather.2
